TPU v7x, 32 devices: a whole 2x2x4 slice. The times are simulated.
32 devices in a mesh: groups: 2 (over y), rows: 4 (over z), shard: 4 (over x, core).
Axes of the slice: x: 2, y: 2, z: 4, core: 2. Of those that a mesh axis runs over, the one named last changes fastest.
Arguments:
- images: bfloat16 [8, 8, 128, 512], P(('groups', 'shard'), 'rows'), parts along dimension 0, may hold values from -6 to 6
- cotangent: bfloat16 [8, 8, 128, 512], P(('groups', 'shard'), 'rows'), parts along dimension 0, may hold values from -6 to 6
- weight_in: bfloat16 [2, 512, 512], P(None, 'shard'), may hold values from -0.25 to 0.25
- weight_group: bfloat16 [2, 144, 512], P(None, 'shard'), may hold values from -0.5 to 0.5
- weight_out: bfloat16 [2, 512, 512], P(None, 'shard'), may hold values from -0.25 to 0.25
Outputs:
- decoded: bfloat16 [8, 8, 128, 512], P(('groups', 'shard'), 'rows'), parts along dimension 0
- grad_images: bfloat16 [8, 8, 128, 512], P(('groups', 'shard'), 'rows'), parts along dimension 0
- grad_in: float32 [4, 512, 512], P('groups', 'shard'), parts along dimension 0
- grad_group: float32 [4, 144, 512], P('groups', 'shard'), parts along dimension 0
- grad_out: float32 [4, 512, 512], P('groups', 'shard'), parts along dimension 0
There are 2 independent parts, one for each index of `groups`. A program takes and returns all parts, laid end to end along the dimension named above; an argument that names none is the same for every part. Nothing has to cross between parts.
All inputs are finite; a program needn't handle non-finite values.
Results may differ from a plain program's by a relative error of at most 0.02.
Values may be sent and summed in bfloat16 or wider, within the bound.
A program may use at most 128 MiB of HBM per device.

v0:
```python
import math
import jax
import jax.numpy as jnp
from jax import lax
from jax.sharding import PartitionSpec as P

GW = 16


def extended_2(cells, sides, width):
    for axis, dim in sides:
        count = lax.axis_size(axis)
        ends = count - 1
        head = lax.slice_in_dim(cells, 0, width, axis=dim)
        tail = lax.slice_in_dim(cells, cells.shape[dim] - width, cells.shape[dim], axis=dim)
        cells = jnp.concatenate(
            [
                lax.ppermute(tail, axis, [(i, (i + 1) % count) for i in range(ends)]),
                cells,
                lax.ppermute(head, axis, [((i + 1) % count, i) for i in range(ends)]),
            ],
            axis=dim,
        )
    return cells


def silu_slope(preact):
    sigmoid_value = jax.nn.sigmoid(preact)
    return sigmoid_value * (1.0 + preact * (1.0 - sigmoid_value))


def block_kernel(full_group, hidden_width, group_width):
    sub_width = min(hidden_width, 128)
    sections = hidden_width // sub_width
    members = sub_width // group_width
    arranged = full_group.reshape(9, group_width, sections, members, group_width)
    arranged = arranged.transpose(0, 2, 3, 1, 4)
    identity = jnp.eye(members, dtype=full_group.dtype)
    expanded = arranged[:, :, :, :, None, :] * identity[None, None, :, None, :, None]
    return expanded.reshape(9, sections, sub_width, sub_width)


def grouped_taps(padded, kernel, out_rows, out_cols, flipped, pattern):
    summed = None
    for tap_index in range(9):
        row_step = tap_index // 3
        col_step = tap_index % 3
        if flipped:
            row_step = 2 - row_step
            col_step = 2 - col_step
        window = padded[:, row_step : row_step + out_rows, col_step : col_step + out_cols, :]
        window = window.reshape(-1, kernel.shape[1], kernel.shape[2])
        tap_term = jnp.einsum(
            pattern, window, kernel[tap_index], preferred_element_type=jnp.float32
        )
        summed = tap_term if summed is None else summed + tap_term
    return summed


def body(images, cotangent, weight_in, weight_group, weight_out):
    tile_count, height, across, channels = images.shape
    block_count = weight_in.shape[0]
    group_width = GW
    pixels = tile_count * height * across
    current = images.reshape(pixels, channels)
    stored = []
    for block_index in range(block_count):
        full_in, full_group, full_out = (
            lax.all_gather(weight_in[block_index], "shard", axis=0, tiled=True),
            lax.all_gather(weight_group[block_index], "shard", axis=0, tiled=True),
            lax.all_gather(weight_out[block_index], "shard", axis=0, tiled=True),
        )
        hidden_width = full_in.shape[1]
        kernel = block_kernel(full_group, hidden_width, group_width)
        pre_one = jnp.dot(current, full_in, preferred_element_type=jnp.float32)
        hidden_one = (
            jax.nn.silu(pre_one)
            .astype(jnp.bfloat16)
            .reshape(tile_count, height, across, hidden_width)
        )
        haloed = extended_2(hidden_one, (("rows", 1),), 1)
        padded_one = jnp.pad(haloed, ((0, 0), (0, 0), (1, 1), (0, 0)))
        pre_two = grouped_taps(padded_one, kernel, height, across, False, "psi,sio->pso").reshape(
            pixels, hidden_width
        )
        hidden_two = jax.nn.silu(pre_two).astype(jnp.bfloat16)
        pre_three = current.astype(jnp.float32) + jnp.dot(
            hidden_two, full_out, preferred_element_type=jnp.float32
        )
        kept_weights = None
        stored.append((current, pre_one, padded_one, pre_two, hidden_two, pre_three, kept_weights))
        current = jax.nn.silu(pre_three).astype(jnp.bfloat16)
    decoded = current.reshape(images.shape)
    grad_flow = cotangent.reshape(pixels, channels)
    shares = []
    for block_index in reversed(range(block_count)):
        flow_in, pre_one, padded_one, pre_two, hidden_two, pre_three, kept_weights = stored[
            block_index
        ]
        full_in, full_group, full_out = (
            lax.all_gather(weight_in[block_index], "shard", axis=0, tiled=True),
            lax.all_gather(weight_group[block_index], "shard", axis=0, tiled=True),
            lax.all_gather(weight_out[block_index], "shard", axis=0, tiled=True),
        )
        hidden_width = full_in.shape[1]
        kernel = block_kernel(full_group, hidden_width, group_width)
        sections = kernel.shape[1]
        sub_width = kernel.shape[2]
        members = sub_width // group_width
        slope_three = grad_flow.astype(jnp.float32) * silu_slope(pre_three)
        low_three = slope_three.astype(jnp.bfloat16)
        part_out = jnp.einsum(
            "pw,pc->wc", hidden_two, low_three, preferred_element_type=jnp.float32
        )
        slope_two = (
            jnp.einsum("pc,wc->pw", low_three, full_out, preferred_element_type=jnp.float32)
            * silu_slope(pre_two)
        ).astype(jnp.bfloat16)
        slope_sections = slope_two.reshape(pixels, sections, sub_width)
        tap_terms = []
        for tap_index in range(9):
            row_step = tap_index // 3
            col_step = tap_index % 3
            window = padded_one[:, row_step : row_step + height, col_step : col_step + across, :]
            window = window.reshape(pixels, sections, sub_width)
            blockwise = jnp.einsum(
                "psi,pso->sio", window, slope_sections, preferred_element_type=jnp.float32
            )
            blockwise = blockwise.reshape(sections, members, group_width, members, group_width)
            diagonal_part = jnp.diagonal(blockwise, axis1=1, axis2=3)
            tap_terms.append(diagonal_part.transpose(1, 0, 3, 2).reshape(group_width, hidden_width))
        part_group = jnp.stack(tap_terms).reshape(9 * group_width, hidden_width)
        slope_grid = slope_two.reshape(tile_count, height, across, hidden_width)
        padded_slope = jnp.pad(slope_grid, ((0, 0), (2, 2), (1, 1), (0, 0)))
        extended = grouped_taps(padded_slope, kernel, height + 2, across, True, "pso,sio->psi")
        extended = extended.reshape(tile_count, height + 2, across, hidden_width)
        edge_rows = jnp.concatenate([extended[:, :1], extended[:, -1:]], axis=1)
        borders = extended_2(edge_rows.astype(jnp.bfloat16), (("rows", 1),), 1).astype(
            edge_rows.dtype
        )
        back_one = extended[:, 1:-1]
        back_one = back_one.at[:, :1].add(borders[:, :1])
        back_one = back_one.at[:, -1:].add(borders[:, -1:])
        slope_one = (back_one.reshape(pixels, hidden_width) * silu_slope(pre_one)).astype(
            jnp.bfloat16
        )
        part_in = jnp.einsum("pc,pw->cw", flow_in, slope_one, preferred_element_type=jnp.float32)
        grad_flow = (
            slope_three
            + jnp.einsum("pw,cw->pc", slope_one, full_in, preferred_element_type=jnp.float32)
        ).astype(jnp.bfloat16)
        shares.append(
            (
                lax.psum_scatter(
                    part_in.astype(jnp.bfloat16), "shard", scatter_dimension=0, tiled=True
                ).astype(jnp.float32),
                lax.psum_scatter(
                    part_group.astype(jnp.bfloat16), "shard", scatter_dimension=0, tiled=True
                ).astype(jnp.float32),
                lax.psum_scatter(
                    part_out.astype(jnp.bfloat16), "shard", scatter_dimension=0, tiled=True
                ).astype(jnp.float32),
            )
        )
    shares = shares[::-1]
    totals = (
        lax.psum(jnp.stack([entry[0] for entry in shares]).astype(jnp.bfloat16), "rows").astype(
            jnp.float32
        ),
        lax.psum(jnp.stack([entry[1] for entry in shares]).astype(jnp.bfloat16), "rows").astype(
            jnp.float32
        ),
        lax.psum(jnp.stack([entry[2] for entry in shares]).astype(jnp.bfloat16), "rows").astype(
            jnp.float32
        ),
    )
    norm_factor = 1.0 / math.sqrt(pixels * lax.axis_size("rows") * lax.axis_size("shard"))
    grad_images = grad_flow.reshape(images.shape)
    return (
        decoded,
        grad_images,
        totals[0] * norm_factor,
        totals[1] * norm_factor,
        totals[2] * norm_factor,
    )


def solution(mesh):
    placed = (
        P(("groups", "shard"), "rows", None, None),
        P(("groups", "shard"), "rows", None, None),
        P(None, "shard", None),
        P(None, "shard", None),
        P(None, "shard", None),
    )
    return jax.shard_map(
        body,
        mesh=mesh,
        in_specs=placed,
        out_specs=(
            P(("groups", "shard"), "rows", None, None),
            P(("groups", "shard"), "rows", None, None),
            P("groups", "shard", None),
            P("groups", "shard", None),
            P("groups", "shard", None),
        ),
        check_vma=False,
    )
```

profile of v0, /device:TPU:0, one launch (start us, length us, event | category | flops | bytes accessed | tf_op | source)
XLA Modules:
  0.0 434.7 jit_solution(18209110213923368101)
XLA Ops:
  8.9 8.6 %all-gather.1 = bf16[1,512,512]{2,1,0:T(8,128)(2,1)S(1)} all-gather(bf16[1,128,512]{2,1,0:T(8,128)(2,1)S(1)} %get-tuple-element.137), channel_id=3, replica_groups=mesh['groups'=2,'rows'=4,'shard'=4] {'shard'}, dimensions={1}, use_global_device_ids=true | all-gather | bytes 655360 | tf_op jit(solution)/shard_map/all_gather | solution.py:69
  20.6 5.2 %collective-permute-start = (bf16[1,1,128,512]{3,2,1,0:T(8,128)(2,1)}, bf16[1,1,128,512]{3,2,1,0:T(8,128)(2,1)}, u32[]{:S(2)}, u32[]{:S(2)}) collective-permute-start(bf16[1,1,128,512]{3,2,1,0:T(8,128)(2,1)} %get-tuple-element.135), channel_id=1, source_target_pairs={{0,4},{4,8},{8,12},{1,5},{5,9},{9,13},{2,6},{6,10},{10,14},{3,7},{... | collective-permute-start | bytes 393224 | tf_op jit(solution)/shard_map/ppermute | solution.py:18
  27.5 5.9 %all-gather = bf16[1,144,512]{2,0,1:T(2,128)(2,1)S(1)} all-gather(bf16[1,36,512]{2,0,1:T(2,128)(2,1)S(1)} %get-tuple-element.141), channel_id=2, replica_groups=mesh['groups'=2,'rows'=4,'shard'=4] {'shard'}, dimensions={1}, use_global_device_ids=true | all-gather | bytes 184320 | tf_op jit(solution)/shard_map/all_gather | solution.py:70
  36.6 6.0 %all-gather.3 = bf16[1,144,512]{2,0,1:T(2,128)(2,1)S(1)} all-gather(bf16[1,36,512]{2,0,1:T(2,128)(2,1)S(1)} %get-tuple-element.142), channel_id=5, replica_groups=mesh['groups'=2,'rows'=4,'shard'=4] {'shard'}, dimensions={1}, use_global_device_ids=true | all-gather | bytes 184320 | tf_op jit(solution)/shard_map/all_gather | solution.py:70
  45.9 9.3 %all-gather.4 = bf16[1,512,512]{2,1,0:T(8,128)(2,1)} all-gather(bf16[1,128,512]{2,1,0:T(8,128)(2,1)} %get-tuple-element.138), channel_id=6, replica_groups=mesh['groups'=2,'rows'=4,'shard'=4] {'shard'}, dimensions={1}, use_global_device_ids=true | all-gather | bytes 655360 | tf_op jit(solution)/shard_map/all_gather | solution.py:69
  55.2 4.4 %broadcast_multiply_fusion.1 = (bf16[9,4,8,16,8,16]{3,2,5,4,1,0:T(8,128)(2,1)S(1)}, bf16[9,4,8,16,8,16]{3,2,5,4,1,0:T(8,128)(2,1)}) fusion(bf16[8,8]{0,1:T(8,128)(2,1)S(1)} %fusion.107, bf16[9,4,8,16,16]{3,2,4,1,0:T(8,128)(2,1)S(1)} %copy.227, bf16[9,4,8,16,16]{3,2,4,1,0:T(8,128)(2,1)S(1)} %copy.238), kind=kLoop, calls=%fused_computation.19 | loop fusion | flops 1179648 | bytes 2654336 | tf_op jit(solution)/shard_map/mul | solution.py:39
  59.6 9.0 %fusion.109 = (bf16[1,4,8,16,8,16]{3,2,5,4,1,0:T(8,128)(2,1)S(1)}, bf16[1,4,8,16,8,16]{3,2,5,4,1,0:T(8,128)(2,1)S(1)}, bf16[1,4,8,16,8,16]{3,2,5,4,1,0:T(8,128)(...) fusion(bf16[9,4,8,16,8,16]{3,2,5,4,1,0:T(8,128)(2,1)} %get-tupl, ...), kind=kLoop, calls=%fused_computation.285 | loop fusion | bytes 4718592 | tf_op jit(solution)/shard_map/slice | solution.py:54
  70.6 2.6 squeeze.99
  73.2 2.6 squeeze.100
  75.9 2.6 squeeze.101
  78.5 2.6 squeeze.102
  81.1 2.6 squeeze.103
  83.7 2.6 squeeze.104
  86.3 2.6 squeeze.105
  88.9 2.6 squeeze.106
  91.5 8.8 %all-gather.2 = bf16[1,512,512]{2,1,0:T(8,128)(2,1)} all-gather(bf16[1,128,512]{2,1,0:T(8,128)(2,1)} %get-tuple-element.139), channel_id=4, replica_groups=mesh['groups'=2,'rows'=4,'shard'=4] {'shard'}, dimensions={1}, use_global_device_ids=true | all-gather | bytes 655360 | tf_op jit(solution)/shard_map/all_gather | solution.py:71
  143.5 5.2 %collective-permute-start.2 = (bf16[1,1,128,512]{3,2,1,0:T(8,128)(2,1)}, bf16[1,1,128,512]{3,2,1,0:T(8,128)(2,1)}, u32[]{:S(2)}, u32[]{:S(2)}) collective-permute-start(bf16[1,1,128,512]{3,2,1,0:T(8,128)(2,1)} %get-tuple-element.131), channel_id=1, source_target_pairs={{0,4},{4,8},{8,12},{1,5},{5,9},{9,13},{2,6},{6,10},{10,14},{3,7},{... | collective-permute-start | bytes 393224 | tf_op jit(solution)/shard_map/ppermute | solution.py:18
  148.7 7.2 %all-gather.5 = bf16[1,512,512]{2,1,0:T(8,128)(2,1)} all-gather(bf16[1,128,512]{2,1,0:T(8,128)(2,1)S(1)} %copy-done.92), channel_id=7, replica_groups=mesh['groups'=2,'rows'=4,'shard'=4] {'shard'}, dimensions={1}, use_global_device_ids=true | all-gather | bytes 655360 | tf_op jit(solution)/shard_map/all_gather | solution.py:71
  155.9 2.6 squeeze.109
  158.5 2.6 squeeze.111
  161.1 2.6 squeeze.112
  163.7 2.6 squeeze.113
  166.3 2.6 squeeze.114
  168.9 2.8 squeeze.115
  186.2 2.7 convert_multiply_fusion
  223.7 5.2 %collective-permute-start.4 = (bf16[1,1,128,512]{3,2,1,0:T(8,128)(2,1)}, bf16[1,1,128,512]{3,2,1,0:T(8,128)(2,1)}, u32[]{:S(2)}, u32[]{:S(2)}) collective-permute-start(bf16[1,1,128,512]{3,2,1,0:T(8,128)(2,1)} %copy.401), channel_id=1, source_target_pairs={{0,4},{4,8},{8,12},{1,5},{5,9},{9,13},{2,6},{6,10},{10,14},{3,7},{... | collective-permute-start | bytes 393224 | tf_op jit(solution)/shard_map/ppermute | solution.py:18
  291.5 5.4 %collective-permute-start.6 = (bf16[1,1,128,512]{3,2,1,0:T(8,128)(2,1)}, bf16[1,1,128,512]{3,2,1,0:T(8,128)(2,1)}, u32[]{:S(2)}, u32[]{:S(2)}) collective-permute-start(bf16[1,1,128,512]{3,2,1,0:T(8,128)(2,1)} %copy.405), channel_id=1, source_target_pairs={{0,4},{4,8},{8,12},{1,5},{5,9},{9,13},{2,6},{6,10},{10,14},{3,7},{... | collective-permute-start | bytes 393224 | tf_op jit(solution)/shard_map/ppermute | solution.py:18
  330.3 8.6 %fusion.108 = (bf16[40,512]{1,0:T(8,128)(2,1)S(1)}, bf16[40,512]{1,0:T(8,128)(2,1)S(1)}) fusion(bf16[144,512]{1,0:T(8,128)(2,1)} %bitcast.72, bf16[144,512]{1,0:T(8,128)(2,1)S(1)} %bitcast.611), kind=kCustom, calls=%all-reduce-scatter.2 | all-reduce-scatter fusion | flops 163841 | bytes 377344
  340.3 3.7 collective-permute-start.8
  348.4 7.7 %reduce-scatter.21.cloned.1.call-done = bf16[128,512]{1,0:T(8,128)(2,1)} async-done(((bf16[512,512]{1,0:T(8,128)(2,1)}), bf16[128,512]{1,0:T(8,128)(2,1)}) %reduce-scatter.21.cloned.1.call-update) | async-done | bytes 131088
  357.9 23.0 %reduce-scatter.17.cloned.1.call-done = bf16[128,512]{1,0:T(8,128)(2,1)} async-done(((bf16[512,512]{1,0:T(8,128)(2,1)}), bf16[128,512]{1,0:T(8,128)(2,1)}) %reduce-scatter.17.cloned.1.call-update) | async-done | bytes 131088
  383.8 40.3 %all-reduce.12.cloned.1.call-done = (bf16[2,128,512]{1,2,0:T(8,128)(2,1)}, bf16[2,36,512]{2,1,0:T(8,128)(2,1)}, bf16[2,128,512]{1,2,0:T(8,128)(2,1)}) async-done(((bf16[2,128,512]{1,2,0:T(8,128)(2,1)}, bf16[2,36,512]{2,1,0:T(8,128)(2,1)}, bf16[2,128,512]{1,2,0:T(8,128)(2,1)}), (bf16[2,128,512]{1,2,0:T(8,128)(2,1)}, bf16[2,36,512]{2,1,0:T(8,128)(2,1)}, ...) | async-done | bytes 598032 | tf_op jit(solution)/shard_map/psum | solution.py:167
  (570 shorter events, 214.8 us)
Async XLA Ops:
  7.2 10.3 %copy-start.98 = (bf16[1,2,128,512]{3,2,1,0:T(8,128)(2,1)S(1)}, bf16[1,2,128,512]{3,2,1,0:T(8,128)(2,1)}, u32[]{:S(2)}) copy-start(bf16[1,2,128,512]{3,2,1,0:T(8,128)(2,1)} %param.13) | copy-start | bytes 786436
  7.2 339.2 %reduce-scatter.23.cloned.1.call-start = ((), (), s32[]{:S(2)}) async-start(), calls=%async_computation.7 | async-start | bytes 655360
  18.6 14.8 %copy-start = (bf16[256,512]{1,0:T(8,128)(2,1)}, bf16[256,512]{1,0:T(8,128)(2,1)S(1)}, u32[]{:S(2)}) copy-start(bf16[256,512]{1,0:T(8,128)(2,1)S(1)} %get-tuple-element.145) | copy-start | bytes 786436
  18.6 8.1 %copy-start.97 = (bf16[2,128,512]{2,1,0:T(8,128)(2,1)S(1)}, bf16[2,128,512]{2,1,0:T(8,128)(2,1)}, u32[]{:S(2)}) copy-start(bf16[2,128,512]{2,1,0:T(8,128)(2,1)} %param.17) | copy-start | bytes 786436
  18.6 8.8 %copy-start.93 = (bf16[2,36,512]{2,0,1:T(2,128)(2,1)S(1)}, bf16[2,36,512]{2,0,1:T(2,128)(2,1)}, u32[]{:S(2)}) copy-start(bf16[2,36,512]{2,0,1:T(2,128)(2,1)} %param.16) | copy-start | bytes 221188
  19.3 81.0 %collective-permute-start.1 = (bf16[1,1,128,512]{3,2,1,0:T(8,128)(2,1)}, bf16[1,1,128,512]{3,2,1,0:T(8,128)(2,1)}, u32[]{:S(2)}, u32[]{:S(2)}) collective-permute-start(bf16[1,1,128,512]{3,2,1,0:T(8,128)(2,1)} %get-tuple-element.136), channel_id=1, source_target_pairs={{4,0},{8,4},{12,8},{5,1},{9,5},{13,9},{6,2},{10,6},{14,10},{7,3},{... | collective-permute-start | bytes 393224 | tf_op jit(solution)/shard_map/ppermute | solution.py:20
  20.6 79.7 %collective-permute-start = (bf16[1,1,128,512]{3,2,1,0:T(8,128)(2,1)}, bf16[1,1,128,512]{3,2,1,0:T(8,128)(2,1)}, u32[]{:S(2)}, u32[]{:S(2)}) collective-permute-start(bf16[1,1,128,512]{3,2,1,0:T(8,128)(2,1)} %get-tuple-element.135), channel_id=1, source_target_pairs={{0,4},{4,8},{8,12},{1,5},{5,9},{9,13},{2,6},{6,10},{10,14},{3,7},{... | collective-permute-start | bytes 393224 | tf_op jit(solution)/shard_map/ppermute | solution.py:18
  88.9 11.5 %copy-start.1 = (bf16[256,512]{1,0:T(8,128)(2,1)S(1)}, bf16[256,512]{1,0:T(8,128)(2,1)}, u32[]{:S(2)}) copy-start(bf16[256,512]{1,0:T(8,128)(2,1)} %copy-done) | copy-start | bytes 786436
  114.2 7.1 %copy-start.62 = (bf16[1,2,128,512]{3,2,1,0:T(8,128)(2,1)S(1)}, bf16[1,2,128,512]{3,2,1,0:T(8,128)(2,1)}, u32[]{:S(2)}) copy-start(bf16[1,2,128,512]{3,2,1,0:T(8,128)(2,1)} %get-tuple-element.104) | copy-start | bytes 786436
  123.9 7.1 %copy-start.2 = (bf16[256,4,128]{0,2,1:T(8,128)(2,1)S(1)}, bf16[256,4,128]{0,2,1:T(8,128)(2,1)}, u32[]{:S(2)}) copy-start(bf16[256,4,128]{0,2,1:T(8,128)(2,1)} %copy.294) | copy-start | bytes 786436
  140.3 8.4 %copy-start.92 = (bf16[1,128,512]{2,1,0:T(8,128)(2,1)S(1)}, bf16[1,128,512]{2,1,0:T(8,128)(2,1)}, u32[]{:S(2)}) copy-start(bf16[1,128,512]{2,1,0:T(8,128)(2,1)} %get-tuple-element.140) | copy-start | bytes 393220
  142.2 33.0 %collective-permute-start.3 = (bf16[1,1,128,512]{3,2,1,0:T(8,128)(2,1)}, bf16[1,1,128,512]{3,2,1,0:T(8,128)(2,1)}, u32[]{:S(2)}, u32[]{:S(2)}) collective-permute-start(bf16[1,1,128,512]{3,2,1,0:T(8,128)(2,1)} %get-tuple-element.132), channel_id=1, source_target_pairs={{4,0},{8,4},{12,8},{5,1},{9,5},{13,9},{6,2},{10,6},{14,10},{7,3},{... | collective-permute-start | bytes 393224 | tf_op jit(solution)/shard_map/ppermute | solution.py:20
  143.5 31.8 %collective-permute-start.2 = (bf16[1,1,128,512]{3,2,1,0:T(8,128)(2,1)}, bf16[1,1,128,512]{3,2,1,0:T(8,128)(2,1)}, u32[]{:S(2)}, u32[]{:S(2)}) collective-permute-start(bf16[1,1,128,512]{3,2,1,0:T(8,128)(2,1)} %get-tuple-element.131), channel_id=1, source_target_pairs={{0,4},{4,8},{8,12},{1,5},{5,9},{9,13},{2,6},{6,10},{10,14},{3,7},{... | collective-permute-start | bytes 393224 | tf_op jit(solution)/shard_map/ppermute | solution.py:18
  173.7 10.5 %copy-start.48 = (bf16[4,128,128]{1,2,0:T(8,128)(2,1)}, bf16[4,128,128]{1,2,0:T(8,128)(2,1)S(1)}, u32[]{:S(2)}) copy-start(bf16[4,128,128]{1,2,0:T(8,128)(2,1)S(1)} %squeeze.117) | copy-start | bytes 393220
  188.9 8.2 %copy-start.119 = (f32[256,512]{1,0:T(8,128)}, f32[256,512]{1,0:T(8,128)S(1)}, u32[]{:S(2)}) copy-start(f32[256,512]{1,0:T(8,128)S(1)} %get-tuple-element.109) | copy-start | bytes 1572868
  221.0 7.8 %copy-start.76 = (bf16[4,128,128]{2,1,0:T(8,128)(2,1)S(1)}, bf16[4,128,128]{2,1,0:T(8,128)(2,1)}, u32[]{:S(2)}) copy-start(bf16[4,128,128]{2,1,0:T(8,128)(2,1)} %fusion.61) | copy-start | bytes 393220
  221.6 35.3 %collective-permute-start.5 = (bf16[1,1,128,512]{3,2,1,0:T(8,128)(2,1)S(1)}, bf16[1,1,128,512]{3,2,1,0:T(8,128)(2,1)}, u32[]{:S(2)}, u32[]{:S(2)}) collective-permute-start(bf16[1,1,128,512]{3,2,1,0:T(8,128)(2,1)S(1)} %copy.402), channel_id=1, source_target_pairs={{4,0},{8,4},{12,8},{5,1},{9,5},{13,9},{6,2},{10,6},{14,10},{7,3},{... | collective-permute-start | bytes 393224 | tf_op jit(solution)/shard_map/ppermute | solution.py:20
  223.7 33.2 %collective-permute-start.4 = (bf16[1,1,128,512]{3,2,1,0:T(8,128)(2,1)}, bf16[1,1,128,512]{3,2,1,0:T(8,128)(2,1)}, u32[]{:S(2)}, u32[]{:S(2)}) collective-permute-start(bf16[1,1,128,512]{3,2,1,0:T(8,128)(2,1)} %copy.401), channel_id=1, source_target_pairs={{0,4},{4,8},{8,12},{1,5},{5,9},{9,13},{2,6},{6,10},{10,14},{3,7},{... | collective-permute-start | bytes 393224 | tf_op jit(solution)/shard_map/ppermute | solution.py:18
  248.9 4.2 copy-start.112
  248.9 4.8 %copy-start.114 = (bf16[1,16,512]{2,1,0:T(8,128)(2,1)S(1)}, bf16[1,16,512]{2,1,0:T(8,128)(2,1)}, u32[]{:S(2)}) copy-start(bf16[1,16,512]{2,1,0:T(8,128)(2,1)} %stack_reshape.88) | copy-start | bytes 49156
  249.8 97.5 %reduce-scatter.19.cloned.1.call-start = ((), (), s32[]{:S(2)}) async-start(), calls=%async_computation.5 | async-start | bytes 655360
  287.2 9.7 %copy-start.78 = (bf16[4,128,128]{2,1,0:T(8,128)(2,1)S(1)}, bf16[4,128,128]{2,1,0:T(8,128)(2,1)}, u32[]{:S(2)}) copy-start(bf16[4,128,128]{2,1,0:T(8,128)(2,1)} %fusion.79) | copy-start | bytes 393220
  289.5 37.1 %collective-permute-start.7 = (bf16[1,1,128,512]{3,2,1,0:T(8,128)(2,1)}, bf16[1,1,128,512]{3,2,1,0:T(8,128)(2,1)}, u32[]{:S(2)}, u32[]{:S(2)}) collective-permute-start(bf16[1,1,128,512]{3,2,1,0:T(8,128)(2,1)} %copy.406), channel_id=1, source_target_pairs={{4,0},{8,4},{12,8},{5,1},{9,5},{13,9},{6,2},{10,6},{14,10},{7,3},{... | collective-permute-start | bytes 393224 | tf_op jit(solution)/shard_map/ppermute | solution.py:20
  291.5 35.1 %collective-permute-start.6 = (bf16[1,1,128,512]{3,2,1,0:T(8,128)(2,1)}, bf16[1,1,128,512]{3,2,1,0:T(8,128)(2,1)}, u32[]{:S(2)}, u32[]{:S(2)}) collective-permute-start(bf16[1,1,128,512]{3,2,1,0:T(8,128)(2,1)} %copy.405), channel_id=1, source_target_pairs={{0,4},{4,8},{8,12},{1,5},{5,9},{9,13},{2,6},{6,10},{10,14},{3,7},{... | collective-permute-start | bytes 393224 | tf_op jit(solution)/shard_map/ppermute | solution.py:18
  310.3 45.9 %reduce-scatter.21.cloned.1.call-start = ((), (), s32[]{:S(2)}) async-start(), calls=%async_computation.6 | async-start | bytes 655360
  325.9 55.0 %reduce-scatter.17.cloned.1.call-start = ((), (), s32[]{:S(2)}) async-start(), calls=%async_computation.4 | async-start | bytes 655360
  329.2 14.9 %copy-start.117 = (u32[32]{0:T(128)S(1)}, u32[32]{0:T(128)}, u32[]{:S(2)}) copy-start(u32[32]{0:T(128)} %constant.395) | copy-start | bytes 388
  330.2 93.8 %all-reduce.12.cloned.1.call-start = ((), (), s32[]{:S(2)}) async-start(), calls=%async_computation.8 | async-start | bytes 1212416 | tf_op jit(solution)/shard_map/psum | solution.py:167
  339.0 6.3 %collective-permute-start.9 = (bf16[12,512]{1,0:T(8,128)(2,1)S(1)}, bf16[12,512]{1,0:T(8,128)(2,1)S(1)}, u32[]{:S(2)}, u32[]{:S(2)}) collective-permute-start(bf16[12,512]{1,0:T(8,128)(2,1)S(1)} %slice.573), channel_id=1, source_target_pairs={{0,1},{1,2},{2,3},{4,5},{5,6},{6,7},{8,9},{9,10},{10,11},{12,13},{... | collective-permute-start | bytes 36872
  340.3 5.1 %collective-permute-start.8 = (bf16[12,512]{1,0:T(8,128)(2,1)S(1)}, bf16[12,512]{1,0:T(8,128)(2,1)S(1)}, u32[]{:S(2)}, u32[]{:S(2)}) collective-permute-start(bf16[12,512]{1,0:T(8,128)(2,1)S(1)} %slice.572), channel_id=1, source_target_pairs={{0,1},{1,2},{2,3},{4,5},{5,6},{6,7},{8,9},{9,10},{10,11},{12,13},{... | collective-permute-start | bytes 36872
  348.4 34.3 %copy-start.20 = (bf16[1,512,512]{2,1,0:T(8,128)(2,1)S(1)}, bf16[1,512,512]{2,1,0:T(8,128)(2,1)}, u32[]{:S(2)}) copy-start(bf16[1,512,512]{2,1,0:T(8,128)(2,1)} %copy-done.19) | copy-start | bytes 1572868
  348.4 34.3 %copy-start.66 = (f32[256,512]{1,0:T(8,128)S(1)}, f32[256,512]{1,0:T(8,128)}, u32[]{:S(2)}) copy-start(f32[256,512]{1,0:T(8,128)} %copy-done.64) | copy-start | bytes 1572868
  (106 other events, 157.6 us)
Sparse Core Ops, SparseCore 0:
  250.0 21.4 reduce-scatter.22
  310.4 21.4 reduce-scatter.18
  334.5 21.6 reduce-scatter.20
  359.2 21.6 reduce-scatter.16
  383.9 40.0 all-reduce.11
where the time goes:
time: 443 us; the launch traced here: 435 us
  local copies, waits for them, and re-layouts  196 us (44%)
  waiting for transfers between devices  71.1 us (16%)
  blocking collectives  54.5 us (12%)
  matrix products  44.2 us (10%)
  starting transfers between devices  31.5 us (7%)
  other arithmetic  20.9 us (5%)
  between operations  16.9 us (4%)
    reshape x52, local copies, waits for them, and re-layouts, grouped_taps(): window = window.reshape(-1, kernel.shape[1], kernel.shape[2])  52.9 us
    squeeze x18, local copies, waits for them, and re-layouts, grouped_taps(): kernel[tap_index]  42 us
    psum x1, waiting for transfers between devices, body(): lax.psum(jnp.stack([entry[0] for entry in shares]).astype(jnp.bfloat16),...  40.3 us
    unnamed x283, local copies, waits for them, and re-layouts  31.7 us
    unnamed x11, waiting for transfers between devices  30.8 us
    ppermute x4, starting transfers between devices, extended_2(): lax.ppermute(tail, axis, [(i, (i + 1) % count) for i in range(ends)])  21 us
    all_gather x2, blocking collectives, body(): lax.all_gather(weight_in[block_index], 'shard', axis=0, tiled=True)  17.9 us
    dot_general x36, matrix products, grouped_taps(): jnp.einsum(pattern, window, kernel[tap_index], preferred_element_type=jnp...  16.2 us
  transfers between devices with their start and end apart: 15, of which 3 were waited for; matrix products, arithmetic and copies ran while one was open for 38% of the time, Pallas kernels for 0%

commit v1 on v0

--- a/solution.py
+++ b/solution.py
@@ -163,8 +163,12 @@
             )
         )
     shares = shares[::-1]
+
+    def _put_circles(t0):
+        return jnp.sum(lax.all_gather(t0, "rows"), axis=0)
+
     totals = (
-        lax.psum(jnp.stack([entry[0] for entry in shares]).astype(jnp.bfloat16), "rows").astype(
+        _put_circles(jnp.stack([entry[0] for entry in shares]).astype(jnp.bfloat16)).astype(
             jnp.float32
         ),
         lax.psum(jnp.stack([entry[1] for entry in shares]).astype(jnp.bfloat16), "rows").astype(

time: 443 us -> 454 us (1.025)
  waiting for transfers between devices: 71.1 us -> 84.5 us
  local copies, waits for them, and re-layouts: 196 us -> 189 us
    all_gather x0 -> x1, waiting for transfers between devices: none -> 25.8 us  [_put_circles(): return jnp.sum(lax.all_gather(t0, 'rows'), axis=0)]
    unnamed x11 -> x10, waiting for transfers between devices: 30.8 us -> 22.3 us
    unnamed x283 -> x257, local copies, waits for them, and re-layouts: 31.7 us -> 28.6 us
  transfers between devices with their start and end apart: 15 -> 16, of which waited for: 3 -> 3; matrix products, arithmetic and copies ran while one was open for 38% -> 37% of each run, Pallas kernels for 0% -> 0%
where the time goes in v1:
time: 454 us; the launch traced here: 446 us
  local copies, waits for them, and re-layouts  189 us (42%)
  waiting for transfers between devices  84.5 us (19%)
  blocking collectives  54.5 us (12%)
  matrix products  44.2 us (10%)
  starting transfers between devices  31.6 us (7%)
  other arithmetic  25.1 us (6%)
  between operations  17.1 us (4%)
    reshape x52, local copies, waits for them, and re-layouts, grouped_taps(): window = window.reshape(-1, kernel.shape[1], kernel.shape[2])  52.9 us
    squeeze x18, local copies, waits for them, and re-layouts, grouped_taps(): kernel[tap_index]  42 us
    psum x1, waiting for transfers between devices, body(): lax.psum(jnp.stack([entry[1] for entry in shares]).astype(jnp.bfloat16),...  36.4 us
    unnamed x257, local copies, waits for them, and re-layouts  28.6 us
    all_gather x1, waiting for transfers between devices, _put_circles(): return jnp.sum(lax.all_gather(t0, 'rows'), axis=0)  25.8 us
    unnamed x10, waiting for transfers between devices  22.3 us
    ppermute x4, starting transfers between devices, extended_2(): lax.ppermute(tail, axis, [(i, (i + 1) % count) for i in range(ends)])  21 us
    all_gather x2, blocking collectives, body(): lax.all_gather(weight_in[block_index], 'shard', axis=0, tiled=True)  17.9 us
  transfers between devices with their start and end apart: 16, of which 3 were waited for; matrix products, arithmetic and copies ran while one was open for 37% of the time, Pallas kernels for 0%

profile of v1, /device:TPU:0, one launch (start us, length us, event | category | flops | bytes accessed | tf_op | source)
XLA Modules:
  0.0 445.9 jit_solution(1433716358149559118)
XLA Ops:
  8.9 8.6 %all-gather.1 = bf16[1,512,512]{2,1,0:T(8,128)(2,1)S(1)} all-gather(bf16[1,128,512]{2,1,0:T(8,128)(2,1)S(1)} %get-tuple-element.131), channel_id=3, replica_groups=mesh['groups'=2,'rows'=4,'shard'=4] {'shard'}, dimensions={1}, use_global_device_ids=true | all-gather | bytes 655360 | tf_op jit(solution)/shard_map/all_gather | solution.py:69
  20.6 5.2 %collective-permute-start = (bf16[1,1,128,512]{3,2,1,0:T(8,128)(2,1)}, bf16[1,1,128,512]{3,2,1,0:T(8,128)(2,1)}, u32[]{:S(2)}, u32[]{:S(2)}) collective-permute-start(bf16[1,1,128,512]{3,2,1,0:T(8,128)(2,1)} %get-tuple-element.129), channel_id=1, source_target_pairs={{0,4},{4,8},{8,12},{1,5},{5,9},{9,13},{2,6},{6,10},{10,14},{3,7},{... | collective-permute-start | bytes 393224 | tf_op jit(solution)/shard_map/ppermute | solution.py:18
  27.5 5.9 %all-gather = bf16[1,144,512]{2,0,1:T(2,128)(2,1)S(1)} all-gather(bf16[1,36,512]{2,0,1:T(2,128)(2,1)S(1)} %get-tuple-element.135), channel_id=2, replica_groups=mesh['groups'=2,'rows'=4,'shard'=4] {'shard'}, dimensions={1}, use_global_device_ids=true | all-gather | bytes 184320 | tf_op jit(solution)/shard_map/all_gather | solution.py:70
  36.6 6.0 %all-gather.3 = bf16[1,144,512]{2,0,1:T(2,128)(2,1)S(1)} all-gather(bf16[1,36,512]{2,0,1:T(2,128)(2,1)S(1)} %get-tuple-element.136), channel_id=5, replica_groups=mesh['groups'=2,'rows'=4,'shard'=4] {'shard'}, dimensions={1}, use_global_device_ids=true | all-gather | bytes 184320 | tf_op jit(solution)/shard_map/all_gather | solution.py:70
  45.9 9.3 %all-gather.4 = bf16[1,512,512]{2,1,0:T(8,128)(2,1)} all-gather(bf16[1,128,512]{2,1,0:T(8,128)(2,1)} %get-tuple-element.132), channel_id=6, replica_groups=mesh['groups'=2,'rows'=4,'shard'=4] {'shard'}, dimensions={1}, use_global_device_ids=true | all-gather | bytes 655360 | tf_op jit(solution)/shard_map/all_gather | solution.py:69
  55.2 4.4 broadcast_multiply_fusion.1
  59.6 9.0 %fusion.109 = (bf16[1,4,8,16,8,16]{3,2,5,4,1,0:T(8,128)(2,1)S(1)}, bf16[1,4,8,16,8,16]{3,2,5,4,1,0:T(8,128)(2,1)S(1)}, bf16[1,4,8,16,8,16]{3,2,5,4,1,0:T(8,128)(...) fusion(bf16[9,4,8,16,8,16]{3,2,5,4,1,0:T(8,128)(2,1)} %get-tupl, ...), kind=kLoop, calls=%fused_computation.285 | loop fusion | bytes 4718592 | tf_op jit(solution)/shard_map/slice | solution.py:54
  70.6 2.6 squeeze.99
  73.2 2.6 squeeze.100
  75.9 2.6 squeeze.101
  78.5 2.6 squeeze.102
  81.1 2.6 squeeze.103
  83.7 2.6 squeeze.104
  86.3 2.6 squeeze.105
  88.9 2.6 squeeze.106
  91.5 8.8 %all-gather.2 = bf16[1,512,512]{2,1,0:T(8,128)(2,1)} all-gather(bf16[1,128,512]{2,1,0:T(8,128)(2,1)} %get-tuple-element.133), channel_id=4, replica_groups=mesh['groups'=2,'rows'=4,'shard'=4] {'shard'}, dimensions={1}, use_global_device_ids=true | all-gather | bytes 655360 | tf_op jit(solution)/shard_map/all_gather | solution.py:71
  143.6 5.2 %collective-permute-start.2 = (bf16[1,1,128,512]{3,2,1,0:T(8,128)(2,1)}, bf16[1,1,128,512]{3,2,1,0:T(8,128)(2,1)}, u32[]{:S(2)}, u32[]{:S(2)}) collective-permute-start(bf16[1,1,128,512]{3,2,1,0:T(8,128)(2,1)} %get-tuple-element.125), channel_id=1, source_target_pairs={{0,4},{4,8},{8,12},{1,5},{5,9},{9,13},{2,6},{6,10},{10,14},{3,7},{... | collective-permute-start | bytes 393224 | tf_op jit(solution)/shard_map/ppermute | solution.py:18
  148.8 7.2 %all-gather.5 = bf16[1,512,512]{2,1,0:T(8,128)(2,1)} all-gather(bf16[1,128,512]{2,1,0:T(8,128)(2,1)S(1)} %copy-done.92), channel_id=7, replica_groups=mesh['groups'=2,'rows'=4,'shard'=4] {'shard'}, dimensions={1}, use_global_device_ids=true | all-gather | bytes 655360 | tf_op jit(solution)/shard_map/all_gather | solution.py:71
  156.0 2.6 squeeze.109
  158.6 2.6 squeeze.111
  161.2 2.6 squeeze.112
  163.8 2.6 squeeze.113
  166.4 2.6 squeeze.114
  169.0 2.8 squeeze.115
  186.2 2.7 convert_multiply_fusion
  223.6 5.2 %collective-permute-start.4 = (bf16[1,1,128,512]{3,2,1,0:T(8,128)(2,1)}, bf16[1,1,128,512]{3,2,1,0:T(8,128)(2,1)}, u32[]{:S(2)}, u32[]{:S(2)}) collective-permute-start(bf16[1,1,128,512]{3,2,1,0:T(8,128)(2,1)} %copy.389), channel_id=1, source_target_pairs={{0,4},{4,8},{8,12},{1,5},{5,9},{9,13},{2,6},{6,10},{10,14},{3,7},{... | collective-permute-start | bytes 393224 | tf_op jit(solution)/shard_map/ppermute | solution.py:18
  297.8 5.4 %collective-permute-start.6 = (bf16[1,1,128,512]{3,2,1,0:T(8,128)(2,1)}, bf16[1,1,128,512]{3,2,1,0:T(8,128)(2,1)}, u32[]{:S(2)}, u32[]{:S(2)}) collective-permute-start(bf16[1,1,128,512]{3,2,1,0:T(8,128)(2,1)} %copy.393), channel_id=1, source_target_pairs={{0,4},{4,8},{8,12},{1,5},{5,9},{9,13},{2,6},{6,10},{10,14},{3,7},{... | collective-permute-start | bytes 393224 | tf_op jit(solution)/shard_map/ppermute | solution.py:18
  326.8 8.6 %fusion.108 = (bf16[40,512]{1,0:T(8,128)(2,1)S(1)}, bf16[40,512]{1,0:T(8,128)(2,1)S(1)}) fusion(bf16[144,512]{1,0:T(8,128)(2,1)} %bitcast.72, bf16[144,512]{1,0:T(8,128)(2,1)S(1)} %bitcast.607), kind=kCustom, calls=%all-reduce-scatter.2 | all-reduce-scatter fusion | flops 163841 | bytes 377344
  336.8 3.7 collective-permute-start.8
  345.7 22.2 %reduce-scatter.17.cloned.1.call-done = bf16[128,512]{1,0:T(8,128)(2,1)} async-done(((bf16[512,512]{1,0:T(8,128)(2,1)}), bf16[128,512]{1,0:T(8,128)(2,1)}) %reduce-scatter.17.cloned.1.call-update) | async-done | bytes 131088
  370.9 36.4 %all-reduce.12.cloned.1.call-done = (bf16[2,36,512]{2,1,0:T(8,128)(2,1)}, bf16[2,128,512]{2,1,0:T(8,128)(2,1)}) async-done(((bf16[2,36,512]{2,1,0:T(8,128)(2,1)}, bf16[2,128,512]{2,1,0:T(8,128)(2,1)}), (bf16[2,36,512]{2,1,0:T(8,128)(2,1)}, bf16[2,128,512]{2,1,0:T(8,128)(2,1)})) %all-reduce.12.cloned.1.call-update) | async-done | bytes 335888 | tf_op jit(solution)/shard_map/psum | solution.py:174
  410.8 25.8 %all-gather.8.cloned.1.call-done = bf16[4,2,128,512]{3,2,1,0:T(8,128)(2,1)} async-done(((bf16[1,2,128,512]{3,2,1,0:T(8,128)(2,1)}), bf16[4,2,128,512]{3,2,1,0:T(8,128)(2,1)}) %all-gather.8.cloned.1.call-update) | async-done | bytes 1048592 | tf_op jit(solution)/shard_map/all_gather | solution.py:168
  (549 shorter events, 212.4 us)
Async XLA Ops:
  7.2 10.3 %copy-start.97 = (bf16[1,2,128,512]{3,2,1,0:T(8,128)(2,1)S(1)}, bf16[1,2,128,512]{3,2,1,0:T(8,128)(2,1)}, u32[]{:S(2)}) copy-start(bf16[1,2,128,512]{3,2,1,0:T(8,128)(2,1)} %param.13) | copy-start | bytes 786436
  7.2 335.6 %reduce-scatter.15.cloned.1.call-start = ((), (), s32[]{:S(2)}) async-start(), calls=%async_computation.6 | async-start | bytes 655360 | tf_op jit(solution)/shard_map/reduce_scatter | solution.py:160
  18.6 14.8 %copy-start = (bf16[256,512]{1,0:T(8,128)(2,1)}, bf16[256,512]{1,0:T(8,128)(2,1)S(1)}, u32[]{:S(2)}) copy-start(bf16[256,512]{1,0:T(8,128)(2,1)S(1)} %get-tuple-element.139) | copy-start | bytes 786436
  18.6 8.1 %copy-start.96 = (bf16[2,128,512]{2,1,0:T(8,128)(2,1)S(1)}, bf16[2,128,512]{2,1,0:T(8,128)(2,1)}, u32[]{:S(2)}) copy-start(bf16[2,128,512]{2,1,0:T(8,128)(2,1)} %param.17) | copy-start | bytes 786436
  18.6 8.8 %copy-start.93 = (bf16[2,36,512]{2,0,1:T(2,128)(2,1)S(1)}, bf16[2,36,512]{2,0,1:T(2,128)(2,1)}, u32[]{:S(2)}) copy-start(bf16[2,36,512]{2,0,1:T(2,128)(2,1)} %param.16) | copy-start | bytes 221188
  19.3 81.0 %collective-permute-start.1 = (bf16[1,1,128,512]{3,2,1,0:T(8,128)(2,1)}, bf16[1,1,128,512]{3,2,1,0:T(8,128)(2,1)}, u32[]{:S(2)}, u32[]{:S(2)}) collective-permute-start(bf16[1,1,128,512]{3,2,1,0:T(8,128)(2,1)} %get-tuple-element.130), channel_id=1, source_target_pairs={{4,0},{8,4},{12,8},{5,1},{9,5},{13,9},{6,2},{10,6},{14,10},{7,3},{... | collective-permute-start | bytes 393224 | tf_op jit(solution)/shard_map/ppermute | solution.py:20
  20.6 79.7 %collective-permute-start = (bf16[1,1,128,512]{3,2,1,0:T(8,128)(2,1)}, bf16[1,1,128,512]{3,2,1,0:T(8,128)(2,1)}, u32[]{:S(2)}, u32[]{:S(2)}) collective-permute-start(bf16[1,1,128,512]{3,2,1,0:T(8,128)(2,1)} %get-tuple-element.129), channel_id=1, source_target_pairs={{0,4},{4,8},{8,12},{1,5},{5,9},{9,13},{2,6},{6,10},{10,14},{3,7},{... | collective-permute-start | bytes 393224 | tf_op jit(solution)/shard_map/ppermute | solution.py:18
  88.9 11.5 %copy-start.1 = (bf16[256,512]{1,0:T(8,128)(2,1)S(1)}, bf16[256,512]{1,0:T(8,128)(2,1)}, u32[]{:S(2)}) copy-start(bf16[256,512]{1,0:T(8,128)(2,1)} %copy-done) | copy-start | bytes 786436
  114.2 7.2 %copy-start.62 = (bf16[1,2,128,512]{3,2,1,0:T(8,128)(2,1)S(1)}, bf16[1,2,128,512]{3,2,1,0:T(8,128)(2,1)}, u32[]{:S(2)}) copy-start(bf16[1,2,128,512]{3,2,1,0:T(8,128)(2,1)} %get-tuple-element.98) | copy-start | bytes 786436
  124.0 7.1 %copy-start.2 = (bf16[256,4,128]{0,2,1:T(8,128)(2,1)S(1)}, bf16[256,4,128]{0,2,1:T(8,128)(2,1)}, u32[]{:S(2)}) copy-start(bf16[256,4,128]{0,2,1:T(8,128)(2,1)} %copy.289) | copy-start | bytes 786436
  140.4 8.4 %copy-start.92 = (bf16[1,128,512]{2,1,0:T(8,128)(2,1)S(1)}, bf16[1,128,512]{2,1,0:T(8,128)(2,1)}, u32[]{:S(2)}) copy-start(bf16[1,128,512]{2,1,0:T(8,128)(2,1)} %get-tuple-element.134) | copy-start | bytes 393220
  142.3 33.0 %collective-permute-start.3 = (bf16[1,1,128,512]{3,2,1,0:T(8,128)(2,1)}, bf16[1,1,128,512]{3,2,1,0:T(8,128)(2,1)}, u32[]{:S(2)}, u32[]{:S(2)}) collective-permute-start(bf16[1,1,128,512]{3,2,1,0:T(8,128)(2,1)} %get-tuple-element.126), channel_id=1, source_target_pairs={{4,0},{8,4},{12,8},{5,1},{9,5},{13,9},{6,2},{10,6},{14,10},{7,3},{... | collective-permute-start | bytes 393224 | tf_op jit(solution)/shard_map/ppermute | solution.py:20
  143.6 31.8 %collective-permute-start.2 = (bf16[1,1,128,512]{3,2,1,0:T(8,128)(2,1)}, bf16[1,1,128,512]{3,2,1,0:T(8,128)(2,1)}, u32[]{:S(2)}, u32[]{:S(2)}) collective-permute-start(bf16[1,1,128,512]{3,2,1,0:T(8,128)(2,1)} %get-tuple-element.125), channel_id=1, source_target_pairs={{0,4},{4,8},{8,12},{1,5},{5,9},{9,13},{2,6},{6,10},{10,14},{3,7},{... | collective-permute-start | bytes 393224 | tf_op jit(solution)/shard_map/ppermute | solution.py:18
  173.8 10.5 %copy-start.48 = (bf16[4,128,128]{1,2,0:T(8,128)(2,1)}, bf16[4,128,128]{1,2,0:T(8,128)(2,1)S(1)}, u32[]{:S(2)}) copy-start(bf16[4,128,128]{1,2,0:T(8,128)(2,1)S(1)} %squeeze.117) | copy-start | bytes 393220
  189.0 8.2 %copy-start.108 = (f32[256,512]{1,0:T(8,128)}, f32[256,512]{1,0:T(8,128)S(1)}, u32[]{:S(2)}) copy-start(f32[256,512]{1,0:T(8,128)S(1)} %get-tuple-element.103) | copy-start | bytes 1572868
  221.0 7.8 %copy-start.78 = (bf16[4,128,128]{2,1,0:T(8,128)(2,1)S(1)}, bf16[4,128,128]{2,1,0:T(8,128)(2,1)}, u32[]{:S(2)}) copy-start(bf16[4,128,128]{2,1,0:T(8,128)(2,1)} %fusion.61) | copy-start | bytes 393220
  221.6 35.3 %collective-permute-start.5 = (bf16[1,1,128,512]{3,2,1,0:T(8,128)(2,1)S(1)}, bf16[1,1,128,512]{3,2,1,0:T(8,128)(2,1)}, u32[]{:S(2)}, u32[]{:S(2)}) collective-permute-start(bf16[1,1,128,512]{3,2,1,0:T(8,128)(2,1)S(1)} %copy.390), channel_id=1, source_target_pairs={{4,0},{8,4},{12,8},{5,1},{9,5},{13,9},{6,2},{10,6},{14,10},{7,3},{... | collective-permute-start | bytes 393224 | tf_op jit(solution)/shard_map/ppermute | solution.py:20
  223.6 33.2 %collective-permute-start.4 = (bf16[1,1,128,512]{3,2,1,0:T(8,128)(2,1)}, bf16[1,1,128,512]{3,2,1,0:T(8,128)(2,1)}, u32[]{:S(2)}, u32[]{:S(2)}) collective-permute-start(bf16[1,1,128,512]{3,2,1,0:T(8,128)(2,1)} %copy.389), channel_id=1, source_target_pairs={{0,4},{4,8},{8,12},{1,5},{5,9},{9,13},{2,6},{6,10},{10,14},{3,7},{... | collective-permute-start | bytes 393224 | tf_op jit(solution)/shard_map/ppermute | solution.py:18
  248.9 4.8 %copy-start.105 = (bf16[1,16,512]{2,1,0:T(8,128)(2,1)S(1)}, bf16[1,16,512]{2,1,0:T(8,128)(2,1)}, u32[]{:S(2)}) copy-start(bf16[1,16,512]{2,1,0:T(8,128)(2,1)} %stack_reshape.88) | copy-start | bytes 49156
  249.8 93.0 %reduce-scatter.13.cloned.1.call-start = ((), (), s32[]{:S(2)}) async-start(), calls=%async_computation.5 | async-start | bytes 655360 | tf_op jit(solution)/shard_map/reduce_scatter | solution.py:160
  292.6 52.0 %reduce-scatter.19.cloned.1.call-start = ((), (), s32[]{:S(2)}) async-start(), calls=%async_computation.8 | async-start | bytes 655360
  294.6 8.6 %copy-start.77 = (bf16[4,128,128]{2,1,0:T(8,128)(2,1)S(1)}, bf16[4,128,128]{2,1,0:T(8,128)(2,1)}, u32[]{:S(2)}) copy-start(bf16[4,128,128]{2,1,0:T(8,128)(2,1)} %fusion.79) | copy-start | bytes 393220
  295.7 27.4 %collective-permute-start.7 = (bf16[1,1,128,512]{3,2,1,0:T(8,128)(2,1)}, bf16[1,1,128,512]{3,2,1,0:T(8,128)(2,1)}, u32[]{:S(2)}, u32[]{:S(2)}) collective-permute-start(bf16[1,1,128,512]{3,2,1,0:T(8,128)(2,1)} %copy.394), channel_id=1, source_target_pairs={{4,0},{8,4},{12,8},{5,1},{9,5},{13,9},{6,2},{10,6},{14,10},{7,3},{... | collective-permute-start | bytes 393224 | tf_op jit(solution)/shard_map/ppermute | solution.py:20
  297.8 25.3 %collective-permute-start.6 = (bf16[1,1,128,512]{3,2,1,0:T(8,128)(2,1)}, bf16[1,1,128,512]{3,2,1,0:T(8,128)(2,1)}, u32[]{:S(2)}, u32[]{:S(2)}) collective-permute-start(bf16[1,1,128,512]{3,2,1,0:T(8,128)(2,1)} %copy.393), channel_id=1, source_target_pairs={{0,4},{4,8},{8,12},{1,5},{5,9},{9,13},{2,6},{6,10},{10,14},{3,7},{... | collective-permute-start | bytes 393224 | tf_op jit(solution)/shard_map/ppermute | solution.py:18
  321.2 46.7 %reduce-scatter.17.cloned.1.call-start = ((), (), s32[]{:S(2)}) async-start(), calls=%async_computation.7 | async-start | bytes 655360
  325.6 14.9 %copy-start.106 = (u32[32]{0:T(128)S(1)}, u32[32]{0:T(128)}, u32[]{:S(2)}) copy-start(u32[32]{0:T(128)} %constant.397) | copy-start | bytes 388
  326.7 80.6 %all-reduce.12.cloned.1.call-start = ((), (), s32[]{:S(2)}) async-start(), calls=%async_computation.9 | async-start | bytes 688128 | tf_op jit(solution)/shard_map/psum | solution.py:174
  335.4 6.3 %collective-permute-start.9 = (bf16[12,512]{1,0:T(8,128)(2,1)S(1)}, bf16[12,512]{1,0:T(8,128)(2,1)S(1)}, u32[]{:S(2)}, u32[]{:S(2)}) collective-permute-start(bf16[12,512]{1,0:T(8,128)(2,1)S(1)} %slice.573), channel_id=1, source_target_pairs={{0,1},{1,2},{2,3},{4,5},{5,6},{6,7},{8,9},{9,10},{10,11},{12,13},{... | collective-permute-start | bytes 36872
  336.8 5.2 %collective-permute-start.8 = (bf16[12,512]{1,0:T(8,128)(2,1)S(1)}, bf16[12,512]{1,0:T(8,128)(2,1)S(1)}, u32[]{:S(2)}, u32[]{:S(2)}) collective-permute-start(bf16[12,512]{1,0:T(8,128)(2,1)S(1)} %slice.572), channel_id=1, source_target_pairs={{0,1},{1,2},{2,3},{4,5},{5,6},{6,7},{8,9},{9,10},{10,11},{12,13},{... | collective-permute-start | bytes 36872
  344.5 25.3 %copy-start.20 = (bf16[1,512,512]{2,1,0:T(8,128)(2,1)S(1)}, bf16[1,512,512]{2,1,0:T(8,128)(2,1)}, u32[]{:S(2)}) copy-start(bf16[1,512,512]{2,1,0:T(8,128)(2,1)} %copy-done.19) | copy-start | bytes 1572868
  344.5 25.3 %copy-start.66 = (f32[256,512]{1,0:T(8,128)S(1)}, f32[256,512]{1,0:T(8,128)}, u32[]{:S(2)}) copy-start(f32[256,512]{1,0:T(8,128)} %copy-done.64) | copy-start | bytes 1572868
  344.5 92.0 %all-gather.8.cloned.1.call-start = ((), (), s32[]{:S(2)}) async-start(), calls=%async_computation.4 | async-start | bytes 1310720 | tf_op jit(solution)/shard_map/all_gather | solution.py:168
  (96 other events, 135.8 us)
Sparse Core Ops, SparseCore 0:
  250.0 21.4 reduce-scatter.14
  292.7 21.4 reduce-scatter.12
  321.4 21.4 reduce-scatter.18
  346.0 21.8 reduce-scatter.16
  370.7 36.4 all-reduce.11
  408.7 27.7 all-gather.7
